TPU v7x, 32 devices: a whole 2x2x4 slice. The times are simulated.
32 devices in a mesh: dp: 16 (over z, y, core), mp: 2 (over x).
Axes of the slice: x: 2, y: 2, z: 4, core: 2. Of those that a mesh axis runs over, the one named last changes fastest.
Arguments:
- frames: bfloat16 [32, 320, 768], P('dp', None, 'mp'), may hold values from -16 to 16
- segment_ids: int32 [32, 320], P('dp'), may hold values from 0 to 4, as said below
- live: int32 [32, 320], P('dp'), may hold values from 0 to 1, as said below
- conv_weight: bfloat16 [6144, 768], P('dp', 'mp'), may hold values from -0.078125 to 0.078125
- qkv_weight: bfloat16 [768, 3, 768], P('dp', None, 'mp'), may hold values from -0.3125 to 0.3125
- out_weight: bfloat16 [768, 768], P('mp', 'dp'), may hold values from -0.875 to 0.875
- up_weight: bfloat16 [768, 3072], P('dp', 'mp'), may hold values from -0.21875 to 0.21875
- down_weight: bfloat16 [3072, 768], P('mp', 'dp'), may hold values from -0.109375 to 0.109375
- up_bias: float32 [3072], P('mp'), may hold values from -3 to 3
- gains: float32 [3, 768], P(None, 'mp'), may hold values from 0.1 to 1.9
- biases: float32 [8, 768], P(None, 'mp'), may hold values from -3 to 3
- out_grad: bfloat16 [32, 320, 768], P('dp', None, 'mp'), may hold values from -6 to 6
Outputs:
- mixed: bfloat16 [32, 320, 768], P('dp', None, 'mp')
- grad_frames: float32 [32, 320, 768], P('dp', None, 'mp')
- grad_conv: float32 [6144, 768], P('dp', 'mp')
- grad_qkv: float32 [768, 3, 768], P('dp', None, 'mp')
- grad_out: float32 [768, 768], P('mp', 'dp')
- grad_up: float32 [768, 3072], P('dp', 'mp')
- grad_down: float32 [3072, 768], P('mp', 'dp')
- grad_up_bias: float32 [3072], P('mp')
- grad_gains: float32 [3, 768], P(None, 'mp')
- grad_biases: float32 [8, 768], P(None, 'mp')
Inputs may be any that keep to these rules, and one draw needn't show every extreme that they name: `segment_ids`: along each row the ids start at 0 and never fall; a row holds 2 to 4 clips, each with its own id; padding frames, at the row's end, take the id after the last clip's. `live`: 1 exactly on the frames of clips, 0 on the padding at a row's end.
All inputs are finite; a program needn't handle non-finite values.
Results may differ from a plain program's by a relative error of at most 0.02.
Values may be sent and summed in bfloat16 or wider, within the bound.
A program may use at most 192 MiB of HBM per device.

v0:
```python
import functools

import jax
import jax.numpy as jnp
from jax import lax
from jax.experimental import pallas as pl
from jax.experimental.pallas import tpu as pltpu
from jax.sharding import PartitionSpec as P

MESH = pl.DeviceIdType.MESH
F32, BF16 = jnp.float32, jnp.bfloat16
D, H, FF, HD = 768, 384, 1536, 64
R, T, L = 2, 320, 384
NB, GW, NA = 8, 48, 16
TM = 64
EPS = 1e-5
THEIRS, QKV, OUT, UP, DOWN, ALL = 0, 384, 1536, 1920, 3456, 4992
NN = (((1,), (0,)), ((), ()))
NT = (((1,), (1,)), ((), ()))
TN = (((0,), (0,)), ((), ()))

def mm(a, b, dims=NN):
    return lax.dot_general(a, b, dims, preferred_element_type=F32)

def gelu_both(v):
    p = 0.5 + 0.5 * lax.erf(v * 0.7071067811865476)
    return v * p, p + v * (0.3989422804014327 * jnp.exp(-0.5 * v * v))

def tiles(body, count=T // TM, init=0):
    return lax.fori_loop(0, count, body, init)

def cols(start, size=H):
    return pl.ds(pl.multiple_of(start, 128), size)


def at(i, size=TM):
    return pl.ds(pl.multiple_of(i * size, size), size)

class Mid:
    def shift_inputs(self, g):
        rows = at(g, GW)
        for r in range(R):
            xg = self.xt[r, rows, :]
            for a in range(NA):
                sh = (64 - 8 * a) % L
                v = pltpu.roll(xg, sh, axis=1) if sh else xg
                self.x16[a * GW:(a + 1) * GW, r * L:(r + 1) * L] = v.astype(BF16)

    def turn_in(self, dst, r, rows):
        dst[r] = jnp.concatenate([rows, jnp.zeros((L - T, H), F32)], axis=0).T

    def lanes(self, ref, r):
        return jnp.concatenate([ref[r:r + 1, :].astype(F32), jnp.zeros((1, L - T), F32)], axis=1)

    def turn_frames(self):
        for r in range(R):
            self.turn_in(self.xt, r, self.act[0, r, :, self.own].astype(F32))
            self.xt[r] = self.xt[r] * self.lanes(self.live, r)

    def conv_forward(self):

        def group(g, c):
            self.shift_inputs(g)
            w = self.convw[:, at(g, GW), :].reshape(NA * GW, NB * GW)
            y = mm(w, self.x16[...], TN)
            for r in range(R):
                acc = y[0:GW, r * L:(r + 1) * L]
                for b in range(1, NB):
                    acc = acc + pltpu.roll(y[b * GW:(b + 1) * GW, r * L:(r + 1) * L], L - b, axis=1)
                self.ot[r, at(g, GW), :] = acc
            return c
        tiles(group, 8)
    def conv_finish(self, r):
        v = self.ot[r].T[:T] + self.par[3:4, self.own]
        gel, dg = gelu_both(v)
        self.dconv[r] = dg
        self.gc[r, :, self.own] = gel.astype(BF16)

    def norm_first(self, r):
        def tile(i, c):
            v = self.act[0, r, at(i), :].astype(F32) + self.gc[r, at(i), :].astype(F32)
            cen = v - jnp.sum(v, axis=1, keepdims=True) * (1.0 / D)
            inv = lax.rsqrt(jnp.sum(cen * cen, axis=1, keepdims=True) * (1.0 / D) + EPS)
            xh = cen * inv
            n = xh * self.par[0:1, :] + self.par[4:5, :]
            self.xh0[r, at(i), :] = xh
            self.inv0[r, at(i), :] = inv
            self.fn[r, at(i), :] = n
            self.flow[r, at(i), :] = n.astype(BF16)
            return c
        tiles(tile)

    def wall_cols(self, start, size):
        return self.wall[:, :, cols(start, size)].reshape(D, size)

    def wall_rows(self, n, start, size):
        return self.wall[pl.ds(n * 8, 8), :, start:start + size].reshape(H, size)

    def project(self, r):
        def part(c, k):
            bias = self.par[pl.ds(5 + c // 2, 1), self.own] * ((c - 1) * (c - 1)).astype(F32)
            v = mm(self.flow[r], self.wall_cols(QKV + c * H, H)) + bias
            self.qkv[r, :, cols(c * H)] = v.astype(BF16)
            return k
        tiles(part, 3)

    def lane_masks(self):
        lane = lax.broadcasted_iota(jnp.int32, (1, 128), 1)
        return [(lane < HD).astype(F32).astype(BF16), (lane >= HD).astype(F32).astype(BF16)]

    def pair(self, ref, r, p, c=0):
        return ref[r, :, cols(p * 128 + c * H, 128)]

    def attend(self, r):
        masks = self.lane_masks()
        ids = self.lanes(self.seg, r)
        same = jnp.broadcast_to(ids, (128, L)).T[:T, 0:1] == ids[:, :T]

        def step(p, c):
            q, k, v = (self.pair(self.qkv, r, p, i) for i in range(3))
            acc = None
            for h in range(2):
                s = mm(q * masks[h], k, NT) * 0.125
                s = jnp.where(same, s, -1e30)
                w = jnp.exp(s - jnp.max(s, axis=1, keepdims=True))
                pr = (w * (1.0 / jnp.sum(w, axis=1, keepdims=True))).astype(BF16)
                self.big[r * 6 + p * 2 + h, 0:T, 0:T] = pr
                o = mm(pr, v * masks[h])
                acc = o if acc is None else acc + o
            self.ctx[r, :, cols(p * 128, 128)] = acc.astype(BF16)
            return c
        tiles(step, 3)

    def add_attended(self, r, ctx, start):
        def part(n, c):
            self.fn[r, :, cols(n * H)] += mm(ctx, self.wall_rows(n, start, H), NT)
            return c
        tiles(part, 2)

    def norm_second(self, r):
        def tile(i, c):
            v = self.fn[r, at(i), :] + self.par[7:8, :]
            cen = v - jnp.sum(v, axis=1, keepdims=True) * (1.0 / D)
            inv = lax.rsqrt(jnp.sum(cen * cen, axis=1, keepdims=True) * (1.0 / D) + EPS)
            xh = cen * inv
            n = xh * self.par[1:2, :] + self.par[8:9, :]
            self.xh1[r, at(i), :] = xh
            self.inv1[r, at(i), :] = inv
            self.sn[r, at(i), :] = n
            self.slow[r, at(i), :] = n.astype(BF16)
            return c
        tiles(tile)

    def feed_up(self, r):
        def part(n, c):
            u = mm(self.slow[r], self.wall_cols(UP + n * H, H)) + self.ub[pl.ds(n, 1), :]
            gel, dg = gelu_both(u)
            self.hid[r, :, cols(n * H)] = gel.astype(BF16)
            self.dg[r, :, cols(n * H)] = dg.astype(BF16)
            return c
        tiles(part, 4)

    def feed_down(self, r):
        def part(n, c):
            self.b_own[r, :, cols(n * H)] = mm(self.hid[r], self.wall_rows(n, DOWN, FF), NT).astype(BF16)
            return c
        tiles(part, 2)

    def add_sums(self, row, value):
        self.psum[row:row + 1, :] += value

    def norm_third(self, r):
        def tile(i, c):
            v = self.sn[r, at(i), :] + (self.b_own[r, at(i), :].astype(F32) + self.b_peer[r, at(i), :].astype(F32)) + self.par[9:10, :]
            cen = v - jnp.sum(v, axis=1, keepdims=True) * (1.0 / D)
            inv = lax.rsqrt(jnp.sum(cen * cen, axis=1, keepdims=True) * (1.0 / D) + EPS)
            xh = cen * inv
            self.mixf[...] = xh * self.par[2:3, :] + self.par[10:11, :]
            self.mixed[r, at(i), :] = self.mixf[:, self.own].astype(BF16)
            e = self.act[1, r, at(i), :].astype(F32)
            sc = e * self.par[2:3, :]
            ex = e * xh
            m1 = jnp.sum(sc, axis=1, keepdims=True) * (1.0 / D)
            m2 = jnp.sum(sc * xh, axis=1, keepdims=True) * (1.0 / D)
            g = inv * (sc - m1 - xh * m2)
            self.sn[r, at(i), :] = g
            self.gdl[r, at(i), :] = g.astype(BF16)
            sums = [jnp.sum(w, axis=0, keepdims=True) for w in (ex, e, g)]
            return tuple(x + y for x, y in zip(c, sums))
        z = jnp.zeros((1, D), F32)
        s = tiles(tile, init=(z, z, z))
        for row, val in zip((2, 10, 9), s):
            self.add_sums(row, val)

    def feed_backward(self, r):
        def part(n, c):
            gh = mm(self.gdl[r], self.wall_cols(DOWN + n * H, H))
            g = (gh * self.dg[r, :, cols(n * H)].astype(F32)).astype(BF16)
            self.dg[r, :, cols(n * H)] = g
            self.pub[pl.ds(n, 1), :] += jnp.sum(g.astype(F32), axis=0, keepdims=True)
            return c
        tiles(part, 4)

    def feed_back_up(self, r):
        def part(n, c):
            self.a_own[r, :, cols(n * H)] = mm(self.dg[r], self.wall_rows(n, UP, FF), NT).astype(BF16)
            return c
        tiles(part, 2)

    def weight_grad(self, src, other, count, start):
        def part(n, c):
            o = other[:, :, cols(n * H)].reshape(R * T, H)
            g = mm(src[...].reshape(R * T, D), o, TN)
            self.wall[:, :, cols(start + n * H)] = g.reshape(16, 48, H).astype(BF16)
            return c
        tiles(part, count)

    def norm_second_back(self, r):
        def tile(i, c):
            e = self.sn[r, at(i), :] + (self.a_own[r, at(i), :].astype(F32) + self.a_peer[r, at(i), :].astype(F32))
            xh = self.xh1[r, at(i), :]
            sc = e * self.par[1:2, :]
            m1 = jnp.sum(sc, axis=1, keepdims=True) * (1.0 / D)
            m2 = jnp.sum(sc * xh, axis=1, keepdims=True) * (1.0 / D)
            g = self.inv1[r, at(i), :] * (sc - m1 - xh * m2)
            self.sn[r, at(i), :] = g
            self.gal[r, at(i), :] = g.astype(BF16)
            sums = [jnp.sum(w, axis=0, keepdims=True) for w in (e * xh, e, g)]
            return tuple(x + y for x, y in zip(c, sums))
        z = jnp.zeros((1, D), F32)
        s = tiles(tile, init=(z, z, z))
        for row, val in zip((1, 8, 7), s):
            self.add_sums(row, val)

    def attend_back(self, r):
        self.gctx[r] = mm(self.gal[r], self.wall_cols(OUT, H)).astype(BF16)
        masks = self.lane_masks()

        def step(p, c):
            q, k, v = (self.pair(self.qkv, r, p, i) for i in range(3))
            go = self.pair(self.gctx, r, p)
            gq = gk = gv = None
            for h in range(2):
                gom = go * masks[h]
                gp = mm(gom, v, NT)
                pr = self.big[r * 6 + p * 2 + h, 0:T, 0:T]
                pf = pr.astype(F32)
                gs = (pf * (gp - jnp.sum(gp * pf, axis=1, keepdims=True))).astype(BF16)
                a, b, d = mm(gs, k * masks[h]), mm(gs, q * masks[h], TN), mm(pr, gom, TN)
                gq, gk, gv = (a, b, d) if gq is None else (gq + a, gk + b, gv + d)
            for i, w in enumerate((gq * 0.125, gk * 0.125, gv)):
                self.gst[r, :, cols(p * 128 + i * H, 128)] = w.astype(BF16)
            return c
        tiles(step, 3)
        for row, c in ((5, 0), (6, 2)):
            self.psum[row:row + 1, self.own] += jnp.sum(self.gst[r, :, c * H:(c + 1) * H].astype(F32), axis=0, keepdims=True)

    def project_back(self, r):
        po = mm(self.gst[r], self.wall_rows(1 - self.mp, QKV, 1152), NT)
        pw = mm(self.gst[r], self.wall_rows(self.mp, QKV, 1152), NT)
        self.b_own[r, :, 0:H] = po.astype(BF16)
        self.ot[r, 0:T, :] = pw
        so = po * self.par[0:1, self.oth]
        sw = pw * self.par[0:1, self.own]
        s1 = jnp.sum(so + sw, axis=1, keepdims=True)
        s2 = jnp.sum(so * self.xh0[r, :, self.oth] + sw * self.xh0[r, :, self.own], axis=1, keepdims=True)
        lane = lax.broadcasted_iota(jnp.int32, (T, 128), 1)
        st = jnp.where(lane == 0, s1, jnp.where(lane == 1, s2, 0.0))
        self.st[r] = st
        st = jnp.concatenate([st, jnp.zeros((L - T, 128), F32)], axis=0).T
        self.st_own[r] = st[0:8, :]

    def norm_first_back(self, r):
        stp = jnp.concatenate([self.st_peer[r], jnp.zeros((120, L), F32)], axis=0).T[:T]
        self.st[r] += stp
        gain = self.par[0:1, :]

        def tile(i, c):
            g1 = self.sn[r, at(i), :]
            sc1 = g1 * gain
            st = self.st[r, at(i), :]
            m1 = (jnp.sum(sc1, axis=1, keepdims=True) + st[:, 0:1]) * (1.0 / D)
            m2 = (jnp.sum(sc1 * self.xh0[r, at(i), :], axis=1, keepdims=True) + st[:, 1:2]) * (1.0 / D)
            xh = self.xh0[r, at(i), self.own]
            e = self.sn[r, at(i), self.own] + self.ot[r, at(i), :] + self.b_peer[r, at(i), 0:H].astype(F32)
            g = self.inv0[r, at(i), :] * (e * self.par[0:1, self.own] - m1 - xh * m2)
            self.gf[r, at(i), :] = g
            low = (g * self.dconv[r, at(i), :]).astype(BF16)
            lf = low.astype(F32)
            self.dconv[r, at(i), :] = lf
            sums = [jnp.sum(w, axis=0, keepdims=True) for w in (e * xh, e, lf)]
            return tuple(x + y for x, y in zip(c, sums))
        z = jnp.zeros((1, H), F32)
        s = tiles(tile, init=(z, z, z))
        for row, val in zip((0, 4, 3), s):
            self.psum[row:row + 1, self.own] += val
        self.turn_in(self.gt, r, self.dconv[r])

    def shift_grads(self, g):
        for r in range(R):
            gg = self.gt[r, at(g, GW), :]
            for b in range(NB):
                v = pltpu.roll(gg, b, axis=1) if b else gg
                self.g8[b * GW:(b + 1) * GW, r * L:(r + 1) * L] = v.astype(BF16)

    def conv_weight_grad(self, first):
        def group(g, c):
            self.shift_inputs(g)
            self.shift_grads(g)
            gr = mm(self.x16[...], self.g8[...], NT)
            self.big[:, at(g, GW), :] = gr.reshape(NA, GW, NB * GW).astype(BF16)
            return c
        lax.fori_loop(first, first + 2, group, 0)

    def conv_input_grad(self, first):
        def group(g, c):
            self.shift_grads(g)
            w = self.convw[:, at(g, GW), :].reshape(NA * GW, NB * GW)
            z = mm(w, self.g8[...])
            for r in range(R):
                acc = None
                for a in range(NA):
                    sh = (8 * a - 64) % L
                    v = z[a * GW:(a + 1) * GW, r * L:(r + 1) * L]
                    v = pltpu.roll(v, sh, axis=1) if sh else v
                    acc = v if acc is None else acc + v
                self.ot[r, at(g, GW), :] = acc
            return c
        lax.fori_loop(first, first + 2, group, 0)

    def add_input_grad(self):
        for r in range(R):
            self.gf[r] += (self.ot[r] * self.lanes(self.live, r)).T[:T]

    def put(self, i, t, v):
        rows = at(t, 16)
        if i == 4:
            for c in range(3):
                self.gqkv[c, rows, :] = v[:, c * H:(c + 1) * H]
            self.gout[rows, :] = v[:, 3 * H:4 * H]
        elif i == 5:
            self.gup[rows, :] = v
        else:
            self.gdown[rows, :] = v


def swap_blocks(x, buf):
    lane = lax.broadcasted_iota(jnp.int32, (GW, H), 1)
    for d in range(8):
        turned = pltpu.roll(x, GW * d, axis=1) if d else x
        for p in range(8):
            q = (p - d) % 8
            rows = turned[GW * p:GW * (p + 1), :]
            if d:
                rows = jnp.where((lane >= GW * p) & (lane < GW * (p + 1)), rows, buf[GW * q:GW * (q + 1), :])
            buf[GW * q:GW * (q + 1), :] = rows


class Ring:
    def __init__(self, n, m, sems):
        self.n, self.m = n, m
        (self.gas, self.gar, self.gbs, self.gbr, self.gss, self.gsr, self.sas, self.sar, self.sbs, self.sbr, self.sss, self.ssr) = sems
        me = lax.axis_index("dp")
        core = lax.rem(me, 2)
        chip = me // 2
        odd = lax.rem(chip, 2)
        half = chip // 2
        self.me, self.core, self.step = me, core, 1 - 2 * core
        self.pos = (1 - odd) * half + odd * (n - 1 - half)
        self.nxt = self.dev(self.step, core)
        self.prv = self.dev(-self.step, core)
        self.sib = me + self.step
        conv = lambda q: lambda d, w=m.convw: w.at[d, 96 * q:96 * (q + 1), :]
        self.views = [conv(q) for q in range(4)] + [
            lambda d: m.wall.at[d, :, 0:UP],
            lambda d: m.wall.at[d, :, UP:DOWN],
            lambda d: m.wall.at[d, :, DOWN:ALL],
            lambda d: m.pall.at[pl.ds(d, 1)],
        ]
        self.out = {}

    def dev(self, k, core):
        n = self.n
        p = lax.rem(self.pos + k + 8 * n, n)
        q = p // (n // 2)
        return 2 * ((1 - q) * 2 * p + q * (2 * (n - 1 - p) + 1)) + core

    def copy(self, src, dst, send, recv, dp):
        return pltpu.make_async_remote_copy(src, dst, send, recv, device_id={"dp": dp}, device_id_type=MESH)

    def go(self, key, copy):
        copy.start()
        self.out.setdefault(key, []).append(copy)

    def sent(self, key):
        for copy in self.out.pop(key):
            copy.wait_send()

    def gather(self, i, s):
        key = ("g", i)
        ahead = (self.gas, self.gar, self.nxt, 4, -self.step, 0)
        back = (self.gbs, self.gbr, self.prv, 3, self.step, 4)
        for send, recv, to, far, way, k in (ahead, back):
            if s > far:
                continue
            slot = self.views[i](self.dev(way * s, self.core))
            if s > 0:
                self.copy(slot, slot, send.at[i, s - 1], recv.at[i, s - 1], to).wait_recv()
            if s < far:
                self.go(key, self.copy(slot, slot, send.at[i, s], recv.at[i, s], to))
            if s > 0 or k == 0:
                self.go(key, self.copy(slot, slot, self.gss.at[i, k + s], self.gsr.at[i, k + s], self.sib))

    def gathered(self, i):
        for k, way in [(s, self.step * s) for s in range(5)] + [(4 + s, -self.step * s) for s in range(1, 4)]:
            slot = self.views[i](self.dev(way, 1 - self.core))
            self.copy(slot, slot, self.gss.at[i, k], self.gsr.at[i, k], self.sib).wait_recv()
        self.sent(("g", i))

    def grads(self, i, d, conv):
        if conv:
            return self.m.big.at[d, at(i, 96), :]
        if i == 4:
            return self.m.wall.at[d, :, QKV:UP]
        return self.views[i](d)

    def slots(self, i, conv):
        m = self.m
        if conv:
            return (lambda k: m.sbc.at[i, k]), (lambda k: m.rrc.at[i, k])
        return m.sb[i].at.__getitem__, m.rr[i].at.__getitem__

    def scatter_begin(self, i, conv=False, wait=False):
        sb, _ = self.slots(i, conv)
        for k, way in ((0, -4), (4, 3), (1, -3), (5, 2), (2, -2), (6, 1), (3, -1), (7, 0)):
            src = self.grads(i, self.dev(way * self.step, 1 - self.core), conv)
            copy = self.copy(src, sb(k), self.sss.at[i, k], self.ssr.at[i, k], self.sib)
            copy.wait_send() if wait else copy.start()

    def scatter(self, i, j, conv=False):
        sb, rr = self.slots(i, conv)
        ahead = (self.sas, self.sar, self.nxt, 4, self.step, 0)
        back = (self.sbs, self.sbr, self.prv, 3, -self.step, 4)
        if j < 4:
            for send, recv, to, far, way, k in (ahead, back):
                if j >= far:
                    continue
                terms = []
                if j > 0:
                    terms.append(rr(k + j - 1))
                    self.copy(terms[0], terms[0], send.at[i, j - 1], recv.at[i, j - 1], to).wait_recv()
                self.add(i, k + j, self.dev(way * (far - j), self.core), terms, sb(k + j), conv)
                self.copy(sb(k + j), rr(k + j), send.at[i, j], recv.at[i, j], to).start()
        else:
            terms = [rr(3), rr(6)]
            self.copy(terms[0], terms[0], self.sas.at[i, 3], self.sar.at[i, 3], self.nxt).wait_recv()
            self.copy(terms[1], terms[1], self.sbs.at[i, 2], self.sbr.at[i, 2], self.prv).wait_recv()
            self.add(i, 7, self.me, terms, None, conv)

    def scattered(self, i, conv=False):
        sb, rr = self.slots(i, conv)
        self.scatter_begin(i, conv, True)
        for send, recv, to, far, k in ((self.sas, self.sar, self.nxt, 4, 0), (self.sbs, self.sbr, self.prv, 3, 4)):
            for j in range(far):
                self.copy(sb(k + j), rr(k + j), send.at[i, j], recv.at[i, j], to).wait_send()

    def add(self, i, k, dev, terms, into, conv):
        held = self.slots(i, conv)[0](k)
        self.copy(held, held, self.sss.at[i, k], self.ssr.at[i, k], self.sib).wait_recv()
        mine = self.grads(i, dev, conv)

        def tile(t, c):
            rows = at(t, 16)
            v = mine[rows, :].astype(F32) + held[rows, :].astype(F32)
            for term in terms:
                v = v + term[rows, :].astype(F32)
            if into is not None:
                into[rows, :] = v.astype(BF16)
            elif conv:
                self.m.xt[0, at(6 * i + t, 16), :] = v
            else:
                self.m.put(i, t, v)
            return c
        tiles(tile, held.shape[0] // 16)


SCRATCH = dict(
    act=((2, R, T, D), BF16), par=((16, D), F32),
    convw=((16, H, H), BF16), wall=((16, 48, ALL), BF16),
    xt=((R, H, L), F32), ot=((R, H, L), F32), gt=((R, H, L), F32), x16=((768, R * L), BF16), g8=((H, R * L), BF16),
    gc=((R, T, D), BF16), dconv=((R, T, H), F32), xh0=((R, T, D), F32), inv0=((R, T, 1), F32), fn=((R, T, D), F32), flow=((R, T, D), BF16),
    qkv=((R, T, 1152), BF16), big=((16, H, H), BF16), ctx=((R, T, H), BF16),
    a_own=((R, T, D), BF16), a_peer=((R, T, D), BF16), b_own=((R, T, D), BF16), b_peer=((R, T, D), BF16),
    xh1=((R, T, D), F32), inv1=((R, T, 1), F32),
    hid=((R, T, FF), BF16), dg=((R, T, FF), BF16), mixf=((TM, D), F32), gdl=((R, T, D), BF16),
    gctx=((R, T, H), BF16), st=((R, T, 128), F32),
    st_own=((R, 8, L), F32), st_peer=((R, 8, L), F32), psum=((16, D), F32), pub=((4, H), F32), ub=((4, H), F32),
)
RING_SCRATCH = dict(pall=((16, 16, H), F32), sbc=((4, 8, 96, H), BF16), rrc=((4, 7, 96, H), BF16))
for _i in range(4, 7):
    RING_SCRATCH["sb%d" % _i] = ((8, 48, FF), BF16)
    RING_SCRATCH["rr%d" % _i] = ((7, 48, FF), BF16)


RING_INS = ("frames", "ograd", "seg", "live", "upb", "gains", "biases", "cw", "qkvw", "outw", "upw", "downw")
RING_OUTS = ("mixed", "gf", "gcw", "gqkv", "gout", "gup", "gdown", "gupb", "ggains", "gbiases")
INS = ("frames", "ograd", "seg", "live", "upb", "gains", "biases", "convw_hbm", "wa_hbm", "wb_hbm")
OUTS = ("mixed", "gf", "gconv_hbm", "ga_hbm", "gb_hbm", "pout")


def layer_kernel(ring, *refs):
    m = Mid()
    names = (RING_INS + RING_OUTS + tuple(SCRATCH) + tuple(RING_SCRATCH)) if ring else (INS + OUTS + tuple(SCRATCH))
    for name, ref in zip(names, refs):
        setattr(m, name, ref)
    loc, snd, rcv = refs[len(names):len(names) + 3]
    m.slow, m.sn, m.gal, m.gst = m.gc, m.fn, m.gdl, m.qkv
    mp = lax.axis_index("mp")
    m.mp = mp
    m.own = pl.ds(pl.multiple_of(mp * H, 128), H)
    m.oth = pl.ds(pl.multiple_of((1 - mp) * H, 128), H)
    peer = {"mp": 1 - mp}
    bar = pltpu.get_barrier_semaphore()
    acts = [pltpu.make_async_copy(x, m.act.at[i, :, :, m.own], loc.at[i]) for i, x in enumerate((m.frames, m.ograd))]
    if ring:
        rg = Ring(8, m, refs[len(names) + 3:])
        m.sb, m.rr = ({i: getattr(m, "%s%d" % (w, i)) for i in range(4, 7)} for w in ("sb", "rr"))
        loads = [pltpu.make_async_copy(m.qkvw.at[c], m.wall.at[rg.me, :, QKV + c * H:QKV + (c + 1) * H], loc.at[2 + c]) for c in range(3)]
        loads += [
            pltpu.make_async_copy(m.outw, m.wall.at[rg.me, :, OUT:UP], loc.at[5]),
            pltpu.make_async_copy(m.upw, m.wall.at[rg.me, :, UP:DOWN], loc.at[6]),
            pltpu.make_async_copy(m.downw, m.wall.at[rg.me, :, DOWN:ALL], loc.at[7]),
        ]
        near = [{"dp": rg.nxt}, {"dp": rg.prv}, {"dp": rg.sib}, peer]
    else:
        loads = [
            pltpu.make_async_copy(m.convw_hbm, m.convw, loc.at[2]),
            pltpu.make_async_copy(m.wa_hbm, m.wall.at[:, :, 0:UP], loc.at[3]),
            pltpu.make_async_copy(m.wb_hbm, m.wall.at[:, :, UP:ALL], loc.at[4]),
        ]
        near = [peer]
    for d in near:
        pl.semaphore_signal(bar, inc=1, device_id=d, device_id_type=MESH)
    for c in acts + loads:
        c.start()
    m.par[0:3, m.own] = m.gains[...]
    m.par[3:11, m.own] = m.biases[...]
    m.psum[...] = jnp.zeros((16, D), F32)
    m.pub[...] = jnp.zeros((4, H), F32)
    for k in range(4):
        m.ub[k:k + 1, :] = m.upb[k * H:(k + 1) * H].reshape(1, H)
    if ring:
        swap_blocks(m.cw[...].astype(F32), m.ot.at[0])
        m.convw[rg.me] = m.ot[0].astype(BF16)
    pl.semaphore_wait(bar, len(near))
    if ring:
        for q in range(4):
            rg.gather(q, 0)

    def swap(i, r, src, dst, land):
        c = pltpu.make_async_remote_copy(src, dst, snd.at[i, r], rcv.at[i, r], device_id=peer, device_id_type=MESH)
        c.start()
        return c, pltpu.make_async_remote_copy(land, land, snd.at[i, r], rcv.at[i, r], device_id=peer, device_id_type=MESH)

    pend = {}
    own, oth = m.own, m.oth
    if ring:
        theirs = m.wall.at[rg.me, :, THEIRS:QKV]
        pend[7, 1] = swap(7, 1, m.outw, theirs, theirs)
    pend[7, 0] = swap(7, 0, m.par.at[:, own], m.par.at[:, own], m.par.at[:, oth])
    for i in range(2):
        acts[i].wait()
        pend[6, i] = swap(6, i, m.act.at[i, :, :, own], m.act.at[i, :, :, own], m.act.at[i, :, :, oth])
    def gather(*items):
        if ring:
            for i, s in items:
                rg.gather(i, s)

    def scatter(*items):
        if ring:
            for i, s in items:
                rg.scatter(i, s)

    m.turn_frames()
    if ring:
        G, S = rg.gather, rg.scatter
        for s in range(1, 5):
            for q in range(4):
                G(q, s)
            if s == 3:
                for c in loads:
                    c.wait()
                pend[7, 1][1].wait_recv()
                G(4, 0)
        gather((4, 1), (5, 0), (6, 0))
        for q in range(4):
            rg.gathered(q)
    else:
        for c in loads:
            c.wait()
    m.conv_forward()
    gather((4, 2), (5, 1))
    for r in range(R):
        m.conv_finish(r)
        pend[0, r] = swap(0, r, m.gc.at[r, :, own], m.gc.at[r, :, own], m.gc.at[r, :, oth])
    gather((6, 1))
    pend[7, 0][1].wait_recv()
    pend[6, 0][1].wait_recv()
    pend[0, 0][1].wait_recv()
    m.norm_first(0)
    gather((4, 3))
    pend[0, 1][1].wait_recv()
    m.norm_first(1)
    gather((5, 2), (6, 2), (4, 4))
    if ring:
        rg.gathered(4)
    for r in range(R):
        m.project(r)
        m.attend(r)
        pend[1, r] = swap(1, r, m.ctx.at[r], m.a_peer.at[r, :, 0:H], m.a_peer.at[r, :, 0:H])
        m.add_attended(r, m.ctx[r], OUT)
        gather((5 + r, 3))
    gather((5, 4))
    if ring:
        rg.gathered(5)
    for r in range(R):
        pend[1, r][1].wait_recv()
        m.add_attended(r, m.a_peer[r, :, 0:H], THEIRS)
        pend[0, r][0].wait_send()
        m.norm_second(r)
        m.feed_up(r)
        if ring and r == 0:
            rg.gather(6, 4)
            rg.gathered(6)
        m.feed_down(r)
        pend[2, r] = swap(2, r, m.b_own.at[r], m.b_peer.at[r], m.b_peer.at[r])
    pend[6, 1][1].wait_recv()
    for r in range(R):
        pend[2, r][1].wait_recv()
        m.norm_third(r)
        m.feed_backward(r)
        if r == 1:
            m.weight_grad(m.gdl, m.hid, 4, DOWN)
            if ring:
                rg.scatter_begin(6)
        pend[1, r][0].wait_send()
        m.feed_back_up(r)
        pend[3, r] = swap(3, r, m.a_own.at[r], m.a_peer.at[r], m.a_peer.at[r])
    scatter((6, 0))
    m.weight_grad(m.slow, m.dg, 4, UP)
    if ring:
        rg.scatter_begin(5)
    else:
        gb = pltpu.make_async_copy(m.wall.at[:, :, UP:ALL], m.gb_hbm, loc.at[4])
        gb.start()
    for r in range(R):
        pend[3, r][1].wait_recv()
        m.norm_second_back(r)
        if r == 0:
            scatter((5, 0))
        m.attend_back(r)
        scatter(((6, 1), (5, 2))[r])
        pend[2, r][0].wait_send()
        m.project_back(r)
        pend[4, r] = swap(4, r, m.b_own.at[r, :, 0:H], m.b_peer.at[r, :, 0:H], m.b_peer.at[r, :, 0:H])
        pend[5, r] = swap(5, r, m.st_own.at[r], m.st_peer.at[r], m.st_peer.at[r])
        if r == 0:
            scatter((5, 1), (6, 2))
    m.weight_grad(m.gal, m.ctx, 1, OUT)
    m.weight_grad(m.flow, m.gst, 3, QKV)
    if ring:
        rg.scatter_begin(4)
        rg.scatter(6, 3)
    else:
        ga = pltpu.make_async_copy(m.wall.at[:, :, QKV:UP], m.ga_hbm, loc.at[3])
        ga.start()
    for r in range(R):
        pend[5, r][1].wait_recv()
        pend[4, r][1].wait_recv()
        m.norm_first_back(r)
        if r == 0:
            scatter((5, 3), (4, 0))
    if ring:
        m.pall[pl.ds(rg.me, 1), 0:11, :] = m.psum[0:11, own][None]
        m.pall[pl.ds(rg.me, 1), 11:12, :] = jnp.zeros((1, 1, H), F32)
        m.pall[pl.ds(rg.me, 1), 12:16, :] = m.pub[...][None]
        G(7, 0)

        def grads(q, c):
            m.conv_weight_grad(2 * q)
            rg.scatter_begin(q, True)

            @pl.when(q > 0)
            def _():
                S(q - 1, 0, True)
            return c

        def grads_in(q, c):
            m.conv_input_grad(2 * q)
            S(q, 1, True)
            return c

        def hop(j):
            def step(q, c):
                S(q, j, True)
                return c
            tiles(step, 4)

        scatter((6, 4))
        tiles(grads, 4)
        S(3, 0, True)
        scatter((4, 1), (5, 4))
        G(7, 1)
        tiles(grads_in, 4)
        scatter((4, 2))
        G(7, 2)
        hop(2)
        m.add_input_grad()
        scatter((4, 3))
        G(7, 3)
        hop(3)
        scatter((4, 4))
        G(7, 4)
        hop(4)
        rg.gathered(7)
        tot = jnp.sum(m.pall[...], axis=0)
        m.ggains[...] = tot[0:3]
        m.gbiases[...] = tot[3:11]
        for k in range(4):
            m.gupb[k * H:(k + 1) * H] = tot[12 + k]
        swap_blocks(m.xt[0], m.gcw)
        for i in range(4, 7):
            rg.scattered(i)
        for q in range(4):
            rg.scattered(q, True)
    else:
        for g in range(0, 8, 2):
            m.conv_weight_grad(g)
            m.conv_input_grad(g)
        m.add_input_grad()
        gc = pltpu.make_async_copy(m.big, m.gconv_hbm, loc.at[2])
        gc.start()
        m.pout[0:11, :] = m.psum[0:11, own]
        m.pout[11:12, :] = jnp.zeros((1, H), F32)
        m.pout[12:16, :] = m.pub[...]
        for c in (ga, gb, gc):
            c.wait()
    if ring:
        pend[7, 1][0].wait_send()
    for i, r in ((3, 0), (3, 1), (4, 0), (4, 1), (5, 0), (5, 1), (6, 0), (6, 1), (7, 0)):
        pend[i, r][0].wait_send()


def layer(ring, *args):
    vm, hb = pl.BlockSpec(memory_space=pltpu.VMEM), pl.BlockSpec(memory_space=pl.ANY)
    S = jax.ShapeDtypeStruct
    outs = [S((R, T, H), BF16), S((R, T, H), F32)]
    dma = pltpu.SemaphoreType.DMA
    scratch = dict(SCRATCH)
    if ring:
        scratch.update(RING_SCRATCH)
        outs += [S((H, H), F32), S((3, 48, H), F32), S((48, H), F32), S((48, FF), F32), S((48, FF), F32), S((FF,), F32), S((3, H), F32), S((8, H), F32)]
        in_specs, out_specs = [hb] * 2 + [vm] * 6 + [hb] * 4, [vm] * 10
        sems = [dma((8,)), dma((8, R)), dma((8, R))] + [dma((8, w)) for w in (4, 4, 3, 3, 8, 8)] + [dma((7, w)) for w in (4, 4, 3, 3, 8, 8)]
    else:
        outs += [S((16, H, H), BF16), S((16, 48, UP - QKV), BF16), S((16, 48, ALL - UP), BF16), S((16, H), F32)]
        in_specs, out_specs = [hb] * 2 + [vm] * 5 + [hb] * 3, [vm] * 2 + [hb] * 3 + [vm]
        sems = [dma((5,)), dma((8, R)), dma((8, R))]
    return pl.pallas_call(
        functools.partial(layer_kernel, ring),
        out_shape=outs,
        in_specs=in_specs,
        out_specs=out_specs,
        scratch_shapes=[pltpu.VMEM(s, d) for s, d in scratch.values()] + sems,
        compiler_params=pltpu.CompilerParams(collective_id=0, has_side_effects=True, vmem_limit_bytes=63 << 20),
        name="layer",
    )(*args)


def pass_on(*arrays):
    count = len(arrays)

    def kernel(*refs):
        ins, outs, held, sems = refs[:count], refs[count:2 * count], refs[2 * count:3 * count], refs[3 * count]
        loads = [pltpu.make_async_copy(ins[i], held[i], sems.at[0, i]) for i in range(count)]
        stores = [pltpu.make_async_copy(held[i], outs[i], sems.at[1, i]) for i in range(count)]
        for c in loads:
            c.start()
        for i in range(count):
            loads[i].wait()
            stores[i].start()
        for c in stores:
            c.wait()

    hb = pl.BlockSpec(memory_space=pl.ANY)
    return pl.pallas_call(
        kernel,
        out_shape=[jax.ShapeDtypeStruct(a.shape, a.dtype) for a in arrays],
        in_specs=[hb] * count,
        out_specs=[hb] * count,
        scratch_shapes=[pltpu.VMEM(a.shape, a.dtype) for a in arrays] + [pltpu.SemaphoreType.DMA((2, count))],
        name="pass_on",
    )(*arrays)


def taps_in(weight):
    blocks = weight.reshape(-1, 8, 48, 8, 48)
    return blocks.transpose(0, 3, 2, 1, 4).reshape(-1, 384, 384)


def taps_out(grad):
    blocks = grad.reshape(-1, 8, 48, 8, 48)
    return blocks.transpose(0, 3, 2, 1, 4).reshape(-1, 384)


def body(frames, segment_ids, live, conv_weight, qkv_weight, out_weight, up_weight, down_weight,
         up_bias, gains, biases, out_grad):
    common = (frames, out_grad, segment_ids, live, up_bias, gains, biases)
    if conv_weight.shape[0] == 384 and qkv_weight.shape[0] == 48:
        mixed, grad_in, g_conv, g_qkv, g_out, g_up, g_down, g_upb, g_gains, g_biases = pass_on(
            *layer(True, *common, conv_weight, qkv_weight.transpose(1, 0, 2), out_weight.T, up_weight, down_weight.T)
        )
        return (mixed, grad_in, g_conv, g_qkv.transpose(1, 0, 2), g_out.T, g_up, g_down.T, g_upb, g_gains, g_biases)
    theirs = lax.ppermute(out_weight.T, "mp", [(0, 1), (1, 0)])
    wa = jnp.concatenate([theirs, qkv_weight.reshape(-1, 3 * H), out_weight.T], axis=1)
    wb = jnp.concatenate([up_weight, down_weight.T], axis=1)
    convw = taps_in(lax.all_gather(conv_weight, "dp", axis=0, tiled=True))
    wa, wb = (lax.all_gather(w, "dp", axis=0, tiled=True).reshape(16, 48, -1) for w in (wa, wb))
    mixed, grad_in, g_conv, g_a, g_b, sums = layer(False, *common, convw, wa, wb)
    g_conv, g_a, g_b = (
        lax.psum_scatter(g, "dp", scatter_dimension=0, tiled=True).astype(F32)
        for g in (taps_out(g_conv), g_a.reshape(D, -1), g_b.reshape(D, -1))
    )
    sums = lax.psum(sums, "dp")
    return (
        mixed,
        grad_in,
        g_conv,
        g_a[:, : 3 * H].reshape(-1, 3, H),
        g_a[:, 3 * H :].T,
        g_b[:, :FF],
        g_b[:, FF:].T,
        sums[12:16].reshape(FF),
        sums[0:3],
        sums[3:11],
    )


def solution(mesh):
    placed = (
        P("dp", None, "mp"),
        P("dp", None),
        P("dp", None),
        P("dp", "mp"),
        P("dp", None, "mp"),
        P("mp", "dp"),
        P("dp", "mp"),
        P("mp", "dp"),
        P("mp"),
        P(None, "mp"),
        P(None, "mp"),
        P("dp", None, "mp"),
    )
    return jax.shard_map(
        body,
        mesh=mesh,
        in_specs=placed,
        out_specs=(
            P("dp", None, "mp"),
            P("dp", None, "mp"),
            P("dp", "mp"),
            P("dp", None, "mp"),
            P("mp", "dp"),
            P("dp", "mp"),
            P("mp", "dp"),
            P("mp"),
            P(None, "mp"),
            P(None, "mp"),
        ),
        check_vma=False,
    )
```

profile of v0, /device:TPU:0, one launch (start us, length us, event | category | flops | bytes accessed | tf_op | source)
XLA Modules:
  0.0 188.0 jit_solution(13997186650292397106)
XLA Ops:
  0.6 184.3 %layer.1 = (bf16[2,320,384]{2,1,0:T(8,128)(2,1)}, f32[2,320,384]{2,1,0:T(8,128)}, f32[384,384]{1,0:T(8,128)}, f32[3,48,384]{2,1,0:T(8,128)}, f32[48,384]{1,0:T(8...) custom-call(bf16[2,320,384]{2,1,0:T(8,128)(2,1)} %refs_0_.1, ...), custom_call_target="tpu_custom_call" | custom-call | tf_op jit(solution)/shard_map/layer/pallas_call | solution.py:769
  184.9 3.0 %pass_on.1 = (bf16[2,320,384]{2,1,0:T(8,128)(2,1)}, f32[2,320,384]{2,1,0:T(8,128)}, f32[384,384]{1,0:T(8,128)}, f32[3,48,384]{2,1,0:T(8,128)}, f32[48,384]{1,0:T...) custom-call(bf16[2,320,384]{2,1,0:T(8,128)(2,1)} %get-tuple-element., ...), custom_call_target="tpu_custom_call" | custom-call | tf_op jit(solution)/shard_map/pass_on/pallas_call | solution.py:796
where the time goes:
time: 188 us
  Pallas kernels  187 us (99%)
    pallas_call x1, Pallas kernels, layer(): pl.pallas_call(functools.partial(layer_kernel, ring), out_shape=outs, in_...  184 us

commit v1 on v0

--- a/solution.py
+++ b/solution.py
@@ -26,8 +26,8 @@
     p = 0.5 + 0.5 * lax.erf(v * 0.7071067811865476)
     return v * p, p + v * (0.3989422804014327 * jnp.exp(-0.5 * v * v))
 
-def tiles(body, count=T // TM, init=0):
-    return lax.fori_loop(0, count, body, init)
+def tiles(body, count=T // TM, init=0, unroll=1):
+    return lax.fori_loop(0, count, body, init, unroll=unroll)
 
 def cols(start, size=H):
     return pl.ds(pl.multiple_of(start, 128), size)
@@ -158,13 +158,13 @@
             self.hid[r, :, cols(n * H)] = gel.astype(BF16)
             self.dg[r, :, cols(n * H)] = dg.astype(BF16)
             return c
-        tiles(part, 4)
+        tiles(part, 4, unroll=4)
 
     def feed_down(self, r):
         def part(n, c):
             self.b_own[r, :, cols(n * H)] = mm(self.hid[r], self.wall_rows(n, DOWN, FF), NT).astype(BF16)
             return c
-        tiles(part, 2)
+        tiles(part, 2, unroll=2)
 
     def add_sums(self, row, value):
         self.psum[row:row + 1, :] += value
@@ -188,7 +188,7 @@
             sums = [jnp.sum(w, axis=0, keepdims=True) for w in (ex, e, g)]
             return tuple(x + y for x, y in zip(c, sums))
         z = jnp.zeros((1, D), F32)
-        s = tiles(tile, init=(z, z, z))
+        s = tiles(tile, init=(z, z, z), unroll=5)
         for row, val in zip((2, 10, 9), s):
             self.add_sums(row, val)
 
@@ -199,13 +199,13 @@
             self.dg[r, :, cols(n * H)] = g
             self.pub[pl.ds(n, 1), :] += jnp.sum(g.astype(F32), axis=0, keepdims=True)
             return c
-        tiles(part, 4)
+        tiles(part, 4, unroll=4)
 
     def feed_back_up(self, r):
         def part(n, c):
             self.a_own[r, :, cols(n * H)] = mm(self.dg[r], self.wall_rows(n, UP, FF), NT).astype(BF16)
             return c
-        tiles(part, 2)
+        tiles(part, 2, unroll=2)
 
     def weight_grad(self, src, other, count, start):
         def part(n, c):
@@ -251,7 +251,7 @@
             for i, w in enumerate((gq * 0.125, gk * 0.125, gv)):
                 self.gst[r, :, cols(p * 128 + i * H, 128)] = w.astype(BF16)
             return c
-        tiles(step, 3)
+        tiles(step, 3, unroll=3)
         for row, c in ((5, 0), (6, 2)):
             self.psum[row:row + 1, self.own] += jnp.sum(self.gst[r, :, c * H:(c + 1) * H].astype(F32), axis=0, keepdims=True)
 
@@ -291,7 +291,7 @@
             sums = [jnp.sum(w, axis=0, keepdims=True) for w in (e * xh, e, lf)]
             return tuple(x + y for x, y in zip(c, sums))
         z = jnp.zeros((1, H), F32)
-        s = tiles(tile, init=(z, z, z))
+        s = tiles(tile, init=(z, z, z), unroll=5)
         for row, val in zip((0, 4, 3), s):
             self.psum[row:row + 1, self.own] += val
         self.turn_in(self.gt, r, self.dconv[r])
@@ -326,7 +326,7 @@
                     acc = v if acc is None else acc + v
                 self.ot[r, at(g, GW), :] = acc
             return c
-        lax.fori_loop(first, first + 2, group, 0)
+        lax.fori_loop(first, first + 4, group, 0)
 
     def add_input_grad(self):
         for r in range(R):
@@ -496,7 +496,7 @@
     gctx=((R, T, H), BF16), st=((R, T, 128), F32),
     st_own=((R, 8, L), F32), st_peer=((R, 8, L), F32), psum=((16, D), F32), pub=((4, H), F32), ub=((4, H), F32),
 )
-RING_SCRATCH = dict(pall=((16, 16, H), F32), sbc=((4, 8, 96, H), BF16), rrc=((4, 7, 96, H), BF16))
+RING_SCRATCH = dict(cwv=((H, H), BF16), pall=((16, 16, H), F32), sbc=((4, 8, 96, H), BF16), rrc=((4, 7, 96, H), BF16))
 for _i in range(4, 7):
     RING_SCRATCH["sb%d" % _i] = ((8, 48, FF), BF16)
     RING_SCRATCH["rr%d" % _i] = ((7, 48, FF), BF16)
@@ -541,6 +541,9 @@
         near = [peer]
     for d in near:
         pl.semaphore_signal(bar, inc=1, device_id=d, device_id_type=MESH)
+    if ring:
+        taps = pltpu.make_async_copy(m.cw, m.cwv, loc.at[8])
+        taps.start()
     for c in acts + loads:
         c.start()
     m.par[0:3, m.own] = m.gains[...]
@@ -550,7 +553,8 @@
     for k in range(4):
         m.ub[k:k + 1, :] = m.upb[k * H:(k + 1) * H].reshape(1, H)
     if ring:
-        swap_blocks(m.cw[...].astype(F32), m.ot.at[0])
+        taps.wait()
+        swap_blocks(m.cwv[...].astype(F32), m.ot.at[0])
         m.convw[rg.me] = m.ot[0].astype(BF16)
     pl.semaphore_wait(bar, len(near))
     if ring:
@@ -693,33 +697,34 @@
             @pl.when(q > 0)
             def _():
                 S(q - 1, 0, True)
-            return c
-
-        def grads_in(q, c):
-            m.conv_input_grad(2 * q)
-            S(q, 1, True)
-            return c
-
-        def hop(j):
+
+            @pl.when(q == 2)
+            def _():
+                S(4, 1)
+            return c
+
+        def hop(j, first=0, last=4):
             def step(q, c):
                 S(q, j, True)
                 return c
-            tiles(step, 4)
-
-        scatter((6, 4))
+            lax.fori_loop(first, last, step, 0)
+
         tiles(grads, 4)
         S(3, 0, True)
-        scatter((4, 1), (5, 4))
         G(7, 1)
-        tiles(grads_in, 4)
+        hop(1, 0, 2)
+        m.conv_input_grad(0)
+        hop(1, 2, 4)
         scatter((4, 2))
         G(7, 2)
-        hop(2)
-        m.add_input_grad()
+        hop(2, 0, 2)
+        m.conv_input_grad(4)
+        hop(2, 2, 4)
         scatter((4, 3))
         G(7, 3)
+        m.add_input_grad()
         hop(3)
-        scatter((4, 4))
+        scatter((6, 4), (5, 4), (4, 4))
         G(7, 4)
         hop(4)
         rg.gathered(7)
@@ -736,7 +741,8 @@
     else:
         for g in range(0, 8, 2):
             m.conv_weight_grad(g)
-            m.conv_input_grad(g)
+            if g % 4 == 2:
+                m.conv_input_grad(g - 2)
         m.add_input_grad()
         gc = pltpu.make_async_copy(m.big, m.gconv_hbm, loc.at[2])
         gc.start()
@@ -760,8 +766,8 @@
     if ring:
         scratch.update(RING_SCRATCH)
         outs += [S((H, H), F32), S((3, 48, H), F32), S((48, H), F32), S((48, FF), F32), S((48, FF), F32), S((FF,), F32), S((3, H), F32), S((8, H), F32)]
-        in_specs, out_specs = [hb] * 2 + [vm] * 6 + [hb] * 4, [vm] * 10
-        sems = [dma((8,)), dma((8, R)), dma((8, R))] + [dma((8, w)) for w in (4, 4, 3, 3, 8, 8)] + [dma((7, w)) for w in (4, 4, 3, 3, 8, 8)]
+        in_specs, out_specs = [hb] * 2 + [vm] * 5 + [hb] * 5, [vm] * 10
+        sems = [dma((9,)), dma((8, R)), dma((8, R))] + [dma((8, w)) for w in (4, 4, 3, 3, 8, 8)] + [dma((7, w)) for w in (4, 4, 3, 3, 8, 8)]
     else:
         outs += [S((16, H, H), BF16), S((16, 48, UP - QKV), BF16), S((16, 48, ALL - UP), BF16), S((16, H), F32)]
         in_specs, out_specs = [hb] * 2 + [vm] * 5 + [hb] * 3, [vm] * 2 + [hb] * 3 + [vm]

time: 188 us -> 184 us (0.979)
  Pallas kernels: 187 us -> 182 us
    pallas_call x1, Pallas kernels: 184 us -> 179 us  [layer(): pl.pallas_call(functools.partial(layer_kernel, ring), out_shape=outs, in_...]
where the time goes in v1:
time: 184 us; the launch traced here: 183 us
  Pallas kernels  182 us (99%)
    pallas_call x1, Pallas kernels, layer(): pl.pallas_call(functools.partial(layer_kernel, ring), out_shape=outs, in_...  179 us

profile of v1, /device:TPU:0, one launch (start us, length us, event | category | flops | bytes accessed | tf_op | source)
XLA Modules:
  0.0 183.2 jit_solution(10181233337781153537)
XLA Ops:
  0.6 179.4 %layer.1 = (bf16[2,320,384]{2,1,0:T(8,128)(2,1)}, f32[2,320,384]{2,1,0:T(8,128)}, f32[384,384]{1,0:T(8,128)}, f32[3,48,384]{2,1,0:T(8,128)}, f32[48,384]{1,0:T(8...) custom-call(bf16[2,320,384]{2,1,0:T(8,128)(2,1)} %refs_0_.1, ...), custom_call_target="tpu_custom_call" | custom-call | tf_op jit(solution)/shard_map/layer/pallas_call | solution.py:775
  180.1 3.0 %pass_on.1 = (bf16[2,320,384]{2,1,0:T(8,128)(2,1)}, f32[2,320,384]{2,1,0:T(8,128)}, f32[384,384]{1,0:T(8,128)}, f32[3,48,384]{2,1,0:T(8,128)}, f32[48,384]{1,0:T...) custom-call(bf16[2,320,384]{2,1,0:T(8,128)(2,1)} %get-tuple-element., ...), custom_call_target="tpu_custom_call" | custom-call | tf_op jit(solution)/shard_map/pass_on/pallas_call | solution.py:802

commit v2 on v1

--- a/solution.py
+++ b/solution.py
@@ -160,11 +160,8 @@
             return c
         tiles(part, 4, unroll=4)
 
-    def feed_down(self, r):
-        def part(n, c):
-            self.b_own[r, :, cols(n * H)] = mm(self.hid[r], self.wall_rows(n, DOWN, FF), NT).astype(BF16)
-            return c
-        tiles(part, 2, unroll=2)
+    def feed_down(self, r, n):
+        self.b_own[r, :, n * H:(n + 1) * H] = mm(self.hid[r], self.wall_rows(n, DOWN, FF), NT).astype(BF16)
 
     def add_sums(self, row, value):
         self.psum[row:row + 1, :] += value
@@ -255,10 +252,11 @@
         for row, c in ((5, 0), (6, 2)):
             self.psum[row:row + 1, self.own] += jnp.sum(self.gst[r, :, c * H:(c + 1) * H].astype(F32), axis=0, keepdims=True)
 
-    def project_back(self, r):
+    def project_back(self, r, send):
         po = mm(self.gst[r], self.wall_rows(1 - self.mp, QKV, 1152), NT)
+        self.b_own[r, :, 0:H] = po.astype(BF16)
+        send()
         pw = mm(self.gst[r], self.wall_rows(self.mp, QKV, 1152), NT)
-        self.b_own[r, :, 0:H] = po.astype(BF16)
         self.ot[r, 0:T, :] = pw
         so = po * self.par[0:1, self.oth]
         sw = pw * self.par[0:1, self.own]
@@ -477,7 +475,7 @@
             if into is not None:
                 into[rows, :] = v.astype(BF16)
             elif conv:
-                self.m.xt[0, at(6 * i + t, 16), :] = v
+                self.m.gcw[at(6 * i + t, 16), :] = v
             else:
                 self.m.put(i, t, v)
             return c
@@ -485,6 +483,7 @@
 
 
 SCRATCH = dict(
+    mixed=((R, T, H), BF16), gf=((R, T, H), F32),
     act=((2, R, T, D), BF16), par=((16, D), F32),
     convw=((16, H, H), BF16), wall=((16, 48, ALL), BF16),
     xt=((R, H, L), F32), ot=((R, H, L), F32), gt=((R, H, L), F32), x16=((768, R * L), BF16), g8=((H, R * L), BF16),
@@ -503,9 +502,9 @@
 
 
 RING_INS = ("frames", "ograd", "seg", "live", "upb", "gains", "biases", "cw", "qkvw", "outw", "upw", "downw")
-RING_OUTS = ("mixed", "gf", "gcw", "gqkv", "gout", "gup", "gdown", "gupb", "ggains", "gbiases")
+RING_OUTS = ("mixed_hbm", "gf_hbm", "gcw", "gqkv", "gout", "gup", "gdown", "gupb", "ggains", "gbiases")
 INS = ("frames", "ograd", "seg", "live", "upb", "gains", "biases", "convw_hbm", "wa_hbm", "wb_hbm")
-OUTS = ("mixed", "gf", "gconv_hbm", "ga_hbm", "gb_hbm", "pout")
+OUTS = ("mixed_hbm", "gf_hbm", "gconv_hbm", "ga_hbm", "gb_hbm", "pout")
 
 
 def layer_kernel(ring, *refs):
@@ -636,11 +635,14 @@
         if ring and r == 0:
             rg.gather(6, 4)
             rg.gathered(6)
-        m.feed_down(r)
-        pend[2, r] = swap(2, r, m.b_own.at[r], m.b_peer.at[r], m.b_peer.at[r])
+        for n in range(2):
+            half = slice(n * H, (n + 1) * H)
+            m.feed_down(r, n)
+            pend[(2, 8)[n], r] = swap((2, 8)[n], r, m.b_own.at[r, :, half], m.b_peer.at[r, :, half], m.b_peer.at[r, :, half])
     pend[6, 1][1].wait_recv()
     for r in range(R):
         pend[2, r][1].wait_recv()
+        pend[8, r][1].wait_recv()
         m.norm_third(r)
         m.feed_backward(r)
         if r == 1:
@@ -650,6 +652,8 @@
         pend[1, r][0].wait_send()
         m.feed_back_up(r)
         pend[3, r] = swap(3, r, m.a_own.at[r], m.a_peer.at[r], m.a_peer.at[r])
+    done = [pltpu.make_async_copy(m.mixed, m.mixed_hbm, loc.at[0])]
+    done[0].start()
     scatter((6, 0))
     m.weight_grad(m.slow, m.dg, 4, UP)
     if ring:
@@ -665,8 +669,12 @@
         m.attend_back(r)
         scatter(((6, 1), (5, 2))[r])
         pend[2, r][0].wait_send()
-        m.project_back(r)
-        pend[4, r] = swap(4, r, m.b_own.at[r, :, 0:H], m.b_peer.at[r, :, 0:H], m.b_peer.at[r, :, 0:H])
+        pend[8, r][0].wait_send()
+
+        def send(r=r):
+            pend[4, r] = swap(4, r, m.b_own.at[r, :, 0:H], m.b_peer.at[r, :, 0:H], m.b_peer.at[r, :, 0:H])
+
+        m.project_back(r, send)
         pend[5, r] = swap(5, r, m.st_own.at[r], m.st_peer.at[r], m.st_peer.at[r])
         if r == 0:
             scatter((5, 1), (6, 2))
@@ -723,6 +731,8 @@
         scatter((4, 3))
         G(7, 3)
         m.add_input_grad()
+        done.append(pltpu.make_async_copy(m.gf, m.gf_hbm, loc.at[1]))
+        done[1].start()
         hop(3)
         scatter((6, 4), (5, 4), (4, 4))
         G(7, 4)
@@ -733,7 +743,6 @@
         m.gbiases[...] = tot[3:11]
         for k in range(4):
             m.gupb[k * H:(k + 1) * H] = tot[12 + k]
-        swap_blocks(m.xt[0], m.gcw)
         for i in range(4, 7):
             rg.scattered(i)
         for q in range(4):
@@ -744,6 +753,8 @@
             if g % 4 == 2:
                 m.conv_input_grad(g - 2)
         m.add_input_grad()
+        done.append(pltpu.make_async_copy(m.gf, m.gf_hbm, loc.at[1]))
+        done[1].start()
         gc = pltpu.make_async_copy(m.big, m.gconv_hbm, loc.at[2])
         gc.start()
         m.pout[0:11, :] = m.psum[0:11, own]
@@ -753,6 +764,8 @@
             c.wait()
     if ring:
         pend[7, 1][0].wait_send()
+    for c in done:
+        c.wait()
     for i, r in ((3, 0), (3, 1), (4, 0), (4, 1), (5, 0), (5, 1), (6, 0), (6, 1), (7, 0)):
         pend[i, r][0].wait_send()
 
@@ -766,12 +779,12 @@
     if ring:
         scratch.update(RING_SCRATCH)
         outs += [S((H, H), F32), S((3, 48, H), F32), S((48, H), F32), S((48, FF), F32), S((48, FF), F32), S((FF,), F32), S((3, H), F32), S((8, H), F32)]
-        in_specs, out_specs = [hb] * 2 + [vm] * 5 + [hb] * 5, [vm] * 10
-        sems = [dma((9,)), dma((8, R)), dma((8, R))] + [dma((8, w)) for w in (4, 4, 3, 3, 8, 8)] + [dma((7, w)) for w in (4, 4, 3, 3, 8, 8)]
+        in_specs, out_specs = [hb] * 2 + [vm] * 5 + [hb] * 5, [hb] * 2 + [vm] * 8
+        sems = [dma((9,)), dma((9, R)), dma((9, R))] + [dma((8, w)) for w in (4, 4, 3, 3, 8, 8)] + [dma((7, w)) for w in (4, 4, 3, 3, 8, 8)]
     else:
         outs += [S((16, H, H), BF16), S((16, 48, UP - QKV), BF16), S((16, 48, ALL - UP), BF16), S((16, H), F32)]
-        in_specs, out_specs = [hb] * 2 + [vm] * 5 + [hb] * 3, [vm] * 2 + [hb] * 3 + [vm]
-        sems = [dma((5,)), dma((8, R)), dma((8, R))]
+        in_specs, out_specs = [hb] * 2 + [vm] * 5 + [hb] * 3, [hb] * 5 + [vm]
+        sems = [dma((5,)), dma((9, R)), dma((9, R))]
     return pl.pallas_call(
         functools.partial(layer_kernel, ring),
         out_shape=outs,
@@ -787,14 +800,19 @@
     count = len(arrays)
 
     def kernel(*refs):
-        ins, outs, held, sems = refs[:count], refs[count:2 * count], refs[2 * count:3 * count], refs[3 * count]
+        ins, outs, held, sems = refs[:count], refs[count:2 * count], refs[2 * count:3 * count], refs[3 * count + 1]
+        turned = refs[3 * count]
         loads = [pltpu.make_async_copy(ins[i], held[i], sems.at[0, i]) for i in range(count)]
-        stores = [pltpu.make_async_copy(held[i], outs[i], sems.at[1, i]) for i in range(count)]
+        stores = [pltpu.make_async_copy(turned if i == 2 else held[i], outs[i], sems.at[1, i]) for i in range(count)]
         for c in loads:
             c.start()
         for i in range(count):
-            loads[i].wait()
-            stores[i].start()
+            if i != 2:
+                loads[i].wait()
+                stores[i].start()
+        loads[2].wait()
+        swap_blocks(held[2][...], turned)
+        stores[2].start()
         for c in stores:
             c.wait()
 
@@ -804,7 +822,7 @@
         out_shape=[jax.ShapeDtypeStruct(a.shape, a.dtype) for a in arrays],
         in_specs=[hb] * count,
         out_specs=[hb] * count,
-        scratch_shapes=[pltpu.VMEM(a.shape, a.dtype) for a in arrays] + [pltpu.SemaphoreType.DMA((2, count))],
+        scratch_shapes=[pltpu.VMEM(a.shape, a.dtype) for a in arrays] + [pltpu.VMEM((H, H), F32), pltpu.SemaphoreType.DMA((2, count))],
         name="pass_on",
     )(*arrays)
 

time: 184 us -> 182 us (0.989)
    pallas_call x1, Pallas kernels: 179 us -> 177 us  [layer(): pl.pallas_call(functools.partial(layer_kernel, ring), out_shape=outs, in_...]
where the time goes in v2:
time: 182 us
  Pallas kernels  181 us (99%)
    pallas_call x1, Pallas kernels, layer(): pl.pallas_call(functools.partial(layer_kernel, ring), out_shape=outs, in_...  177 us
    pallas_call x1, Pallas kernels, pass_on(): pl.pallas_call(kernel, out_shape=[jax.ShapeDtypeStruct(a.shape, a.dtype)...  3.65 us

profile of v2, /device:TPU:0, one launch (start us, length us, event | category | flops | bytes accessed | tf_op | source)
XLA Modules:
  0.0 181.6 jit_solution(99961920635113269)
XLA Ops:
  0.6 177.1 %layer.1 = (bf16[2,320,384]{2,1,0:T(8,128)(2,1)}, f32[2,320,384]{2,1,0:T(8,128)}, f32[384,384]{1,0:T(8,128)}, f32[3,48,384]{2,1,0:T(8,128)}, f32[48,384]{1,0:T(8...) custom-call(bf16[2,320,384]{2,1,0:T(8,128)(2,1)} %refs_0_.1, ...), custom_call_target="tpu_custom_call" | custom-call | tf_op jit(solution)/shard_map/layer/pallas_call | solution.py:788
  177.7 3.6 %pass_on.1 = (bf16[2,320,384]{2,1,0:T(8,128)(2,1)}, f32[2,320,384]{2,1,0:T(8,128)}, f32[384,384]{1,0:T(8,128)}, f32[3,48,384]{2,1,0:T(8,128)}, f32[48,384]{1,0:T...) custom-call(bf16[2,320,384]{2,1,0:T(8,128)(2,1)} %get-tuple-element., ...), custom_call_target="tpu_custom_call" | custom-call | tf_op jit(solution)/shard_map/pass_on/pallas_call | solution.py:820
